TPU v7x, 32 devices: a whole 2x2x4 slice. The times are simulated.
32 devices in a mesh: groups: 2 (over y), date: 4 (over z), tile: 2 (over x), head: 2 (over core).
Axes of the slice: x: 2, y: 2, z: 4, core: 2. Of those that a mesh axis runs over, the one named last changes fastest.
Arguments:
- tokens: bfloat16 [8, 8, 8, 64, 256], P('groups', 'tile', None, 'date'), parts along dimension 0, may hold values from -240 to 240
- cloud_mask: int32 [8, 8, 8, 64], P('groups', 'tile', None, 'date'), parts along dimension 0, may hold values from 0 to 1, as said below
- day_of_year: int32 [128], P(('groups', 'date')), parts along dimension 0, may hold values from 0 to 1460
- query: float32 [256], P('head'), may hold values from -6 to 6
- key_weight: bfloat16 [256, 256], P(None, 'head'), may hold values from -0.375 to 0.375
- value_weight: bfloat16 [256, 256], P(None, 'head'), may hold values from -0.375 to 0.375
- conv_first: bfloat16 [3, 3, 256, 256], P(None, None, None, 'head'), may hold values from -0.375 to 0.375
- conv_second: bfloat16 [3, 3, 256, 256], P(None, None, None, 'head'), may hold values from -0.1875 to 0.1875
Outputs:
- feature_map: bfloat16 [8, 8, 8, 256], P(('groups', 'date'), 'tile', None, 'head'), parts along dimension 0
There are 2 independent parts, one for each index of `groups`. A program takes and returns all parts, laid end to end along the dimension named above; an argument that names none is the same for every part. Nothing has to cross between parts.
Inputs may be any that keep to these rules, and one draw needn't show every extreme that they name: `cloud_mask`: a pixel may be clouded on all 64 dates.
All inputs are finite; a program needn't handle non-finite values.
Results may differ from a plain program's by a relative error of at most 0.012.
The roundings to bfloat16 on the way count: a program that leaves them out, or rounds other values in their place, can miss the bound.
Values may be sent and summed in bfloat16 or wider, within the bound.
A program may use at most 128 MiB of HBM per device.

v0:
```python
import jax
import jax.numpy as jnp
from jax import lax
from jax.sharding import PartitionSpec as P

HSIZE = 32
TILE_DEV = 1
cloud_penalty = 6.0


def with_halo(block, sides, width):
    for axis, dim in sides:
        count = lax.axis_size(axis)
        forward = [(i, i + 1) for i in range(count - 1)]
        backward = [(target, source) for source, target in forward]
        low = lax.ppermute(
            lax.slice_in_dim(block, block.shape[dim] - width, None, axis=dim), axis, forward
        )
        high = lax.ppermute(lax.slice_in_dim(block, 0, width, axis=dim), axis, backward)
        block = jnp.concatenate([low, block, high], axis=dim)
    return block


def encoding(day_of_year, width):
    chan = jnp.arange(width)
    expo = (2 * (chan // 2)).astype(jnp.float32) / width
    freq = jnp.power(jnp.float32(1000.0), -expo)
    angle = day_of_year.astype(jnp.float32)[:, None] * freq[None, :]
    return jnp.where((chan % 2 == 0)[None, :], jnp.sin(angle), jnp.cos(angle))


def widen(scales):
    return jnp.repeat(scales, HSIZE, axis=-1)


def merge_blocks(tops, tots, parts):
    best = jnp.max(tops, axis=0)
    scales = jnp.exp(tops - best[None])
    own_totals = jnp.sum(tots * scales, axis=0)
    own_sums = jnp.sum(parts * widen(scales), axis=0)
    return (own_totals, own_sums)


def convolve(block, kernel):
    rows, cols = (block.shape[1], block.shape[2])
    padded = with_halo(block, (("tile", 1),), 1)
    whole = lax.all_gather(padded, "head", axis=3, tiled=True)
    whole = jnp.pad(whole, ((0, 0), (0, 0), (1, 1), (0, 0)))
    total = jnp.zeros((block.shape[0] * rows * cols, kernel.shape[3]), jnp.float32)
    for arow in range(3):
        for bcol in range(3):
            piece = whole[:, arow : arow + rows, bcol : bcol + cols, :].reshape(-1, whole.shape[3])
            total = total + jnp.dot(piece, kernel[arow, bcol], preferred_element_type=jnp.float32)
    return total.reshape(block.shape[0], rows, cols, kernel.shape[3])


def local(
    tokens, cloud_mask, day_of_year, query, key_weight, value_weight, conv_first, conv_second
):
    tiles, rows, cols, dates, width = tokens.shape
    heads_dev = query.shape[0] // HSIZE
    table = encoding(day_of_year, width)
    inputs = (
        (tokens.astype(jnp.float32) + table[None, None, None])
        .astype(jnp.bfloat16)
        .reshape(-1, width)
    )
    keys = jnp.dot(inputs, key_weight, preferred_element_type=jnp.float32).reshape(
        tiles, rows, cols, dates, heads_dev, HSIZE
    )
    vals = jnp.dot(inputs, value_weight, preferred_element_type=jnp.float32).reshape(
        tiles, rows, cols, dates, heads_dev, HSIZE
    )
    query_heads = query.reshape(heads_dev, HSIZE)
    score = jnp.sum(keys * query_heads, axis=-1) / jnp.sqrt(jnp.float32(HSIZE))
    score = score - cloud_penalty * (1.0 - cloud_mask[..., None].astype(jnp.float32))
    top = jnp.max(score, axis=3)
    expo = jnp.exp(score - top[:, :, :, None, :])
    totals = jnp.sum(expo, axis=3)
    sums = jnp.sum(expo[..., None] * vals, axis=3).reshape(tiles, rows, cols, heads_dev * HSIZE)
    got = (
        lax.all_to_all(top, "date", split_axis=0, concat_axis=0, tiled=True),
        lax.all_to_all(totals, "date", split_axis=0, concat_axis=0, tiled=True),
        lax.all_to_all(sums, "date", split_axis=0, concat_axis=0, tiled=True),
    )
    sources = got[0].shape[0] // TILE_DEV
    tops = got[0].reshape(sources, TILE_DEV, rows, cols, heads_dev)
    tots = got[1].reshape(sources, TILE_DEV, rows, cols, heads_dev)
    parts = got[2].reshape(sources, TILE_DEV, rows, cols, heads_dev * HSIZE)
    own_totals, own_sums = merge_blocks(tops, tots, parts)
    pooled = (own_sums / widen(own_totals)).astype(jnp.bfloat16)
    hidden = jax.nn.relu(convolve(pooled, conv_first)).astype(jnp.bfloat16)
    return convolve(hidden, conv_second).astype(jnp.bfloat16)


def solution(mesh):
    in_specs = (
        P("groups", "tile", None, "date", None),
        P("groups", "tile", None, "date"),
        P(("groups", "date")),
        P("head"),
        P(None, "head"),
        P(None, "head"),
        P(None, None, None, "head"),
        P(None, None, None, "head"),
    )
    out_specs = P(("groups", "date"), "tile", None, "head")
    return jax.shard_map(local, mesh=mesh, in_specs=in_specs, out_specs=out_specs, check_vma=False)
```

profile of v0, /device:TPU:0, one launch (start us, length us, event | category | flops | bytes accessed | tf_op | source)
XLA Modules:
  0.0 57.5 jit_solution(14288607514884827071)
XLA Ops:
  0.0 0.9 %copy.23 = bf16[256,128]{0,1:T(8,128)(2,1)S(1)} copy(bf16[256,128]{1,0:T(8,128)(2,1)} %param.12) | data formatting | bytes 131072 | tf_op args[4]
  1.0 0.7 %mul.62 = f32[4,32]{1,0:T(4,128)S(1)} reshape(f32[128]{0:T(128)} %param.11) | data formatting | bytes 1024 | tf_op jit(solution)/shard_map/mul | solution.py:75
  1.7 0.7 %convert_element_type.63 = f32[16]{0:T(128)S(1)} convert(s32[16]{0:T(128)} %param.10) | non-fusion elementwise | flops 16 | bytes 128 | tf_op jit(solution)/shard_map/convert_element_type | solution.py:28
  2.4 0.8 %subtract_multiply_fusion = f32[4,4,8,16]{3,2,1,0:T(8,128)S(1)} fusion(s32[4,4,8,16]{3,2,1,0:T(8,128)} %param.9), kind=kLoop, calls=%fused_computation.79 | loop fusion | flops 6144 | bytes 16384 | tf_op jit(solution)/shard_map/mul | solution.py:76
  3.4 2.6 %multiply_reduce_fusion.1 = f32[4,4,8,16,4]{3,4,2,1,0:T(4,128)S(1)} fusion(bf16[4,32,256,1,1,1]{2,1,0,5,4,3:T(8,128)(2,1)S(1)} %bitcast.147, f32[4,32]{1,0:T(4,128)S(1)} %mul.62, bf16[4,4,8,16,256]{4,3,2,1,0:T(8,128)(2,1)} %param.8, f32[16,256]{1,0:T(8,128)S(1)} %fusion.47), kind=kOutput, calls=%fused_computation.1 | convolution fusion | flops 136306688 | bytes 1163776 | tf_op jit(solution)/shard_map/dot_general | solution.py:68
  6.0 0.2 fusion.8
  6.3 0.2 copy.25
  6.4 0.7 %reshape.252 = f32[4,1,128]{2,1,0:T(1,128)} reshape(f32[4,4,4,8]{3,2,1,0:T(4,128)S(1)} %bitcast.146) | data formatting | bytes 4096
  7.1 6.3 %all-to-all-start.1 = ((f32[4,1,128]{2,1,0:T(1,128)}), f32[4,1,128]{2,1,0:T(1,128)S(1)}, u32[]{:S(2)}, u32[]{:S(2)}) async-start(f32[4,1,128]{2,1,0:T(1,128)} %reshape.252), calls=%async_computation.1 | async-start | bytes 4096 | tf_op jit(solution)/shard_map/all_to_all | solution.py:82
  13.4 0.4 fusion.92
  14.0 1.4 %multiply_reduce_fusion = f32[4,4,8,4,32]{4,3,2,1,0:T(4,128)S(1)} fusion(bf16[4,32,256,1,1,1]{2,1,0,5,4,3:T(8,128)(2,1)S(1)} %bitcast.148, f32[4,4,8,16,4]{3,4,2,1,0:T(4,128)S(1)} %get-tuple-element.8, bf16[4,4,8,16,256]{4,3,2,1,0:T(8,128)(2,1)S(1)} %copy-done.3, f32[16,256]{1,0:T(8,128)S(1)} %fusion.47), kind=kOutput, calls=%fused_computation | convolution fusion | flops 136298496 | bytes 1228800 | tf_op jit(solution)/shard_map/dot_general | solution.py:71
  15.6 0.7 %reshape.250 = f32[4,1,128]{2,1,0:T(1,128)} reshape(f32[4,4,4,8]{3,2,1,0:T(4,128)S(1)} %bitcast.145) | data formatting | bytes 4096
  16.2 0.8 %reshape.228 = f32[4,4,8,128]{3,2,1,0:T(8,128)} reshape(f32[4,4,8,4,32]{4,3,2,1,0:T(4,128)S(1)} %multiply_reduce_fusion) | data formatting | bytes 131072 | tf_op jit(solution)/shard_map/reshape | solution.py:80
  17.0 1.9 %all-to-all-done.1 = f32[4,1,128]{2,1,0:T(1,128)S(1)} async-done(((f32[4,1,128]{2,1,0:T(1,128)}), f32[4,1,128]{2,1,0:T(1,128)S(1)}, u32[]{:S(2)}, u32[]{:S(2)}) %all-to-all-start.1) | async-done | bytes 2080 | tf_op jit(solution)/shard_map/all_to_all | solution.py:82
  18.9 3.2 %all-to-all-start.2 = ((f32[4,1,128]{2,1,0:T(1,128)}), f32[4,1,128]{2,1,0:T(1,128)S(1)}, u32[]{:S(2)}, u32[]{:S(2)}) async-start(f32[4,1,128]{2,1,0:T(1,128)} %reshape.250), calls=%async_computation.2 | async-start | bytes 4096 | tf_op jit(solution)/shard_map/all_to_all | solution.py:83
  22.1 0.5 broadcast.137
  22.6 0.7 %reduce.6 = f32[4,128]{1,0:T(4,128)S(1)} reduce(f32[4,1,128]{2,1,0:T(1,128)S(1)} %all-to-all-done.1, f32[]{:T(128)} %broadcast.137), dimensions={1}, to_apply=%all_to_all.10.reduce_sub_computation | reduce | bytes 4100 | tf_op jit(solution)/shard_map/all_to_all | solution.py:82
  23.4 4.1 %all-to-all-done.2 = f32[4,1,128]{2,1,0:T(1,128)S(1)} async-done(((f32[4,1,128]{2,1,0:T(1,128)}), f32[4,1,128]{2,1,0:T(1,128)S(1)}, u32[]{:S(2)}, u32[]{:S(2)}) %all-to-all-start.2) | async-done | bytes 2080 | tf_op jit(solution)/shard_map/all_to_all | solution.py:83
  27.5 3.3 %all-to-all-start = ((f32[4,4,8,128]{3,2,1,0:T(8,128)}), f32[4,4,8,128]{3,2,1,0:T(8,128)S(1)}, u32[]{:S(2)}, u32[]{:S(2)}) async-start(f32[4,4,8,128]{3,2,1,0:T(8,128)} %reshape.228), calls=%async_computation | async-start | bytes 131072 | tf_op jit(solution)/shard_map/all_to_all | solution.py:84
  30.8 0.7 %reduce.7 = f32[4,128]{1,0:T(4,128)S(1)} reduce(f32[4,1,128]{2,1,0:T(1,128)S(1)} %all-to-all-done.2, f32[]{:T(128)} %broadcast.137), dimensions={1}, to_apply=%all_to_all.11.reduce_sub_computation | reduce | bytes 4100 | tf_op jit(solution)/shard_map/all_to_all | solution.py:83
  31.9 0.2 copy.26
  32.1 0.2 broadcast_in_dim.27
  32.5 4.1 %all-to-all-done = f32[4,4,8,128]{3,2,1,0:T(8,128)S(1)} async-done(((f32[4,4,8,128]{3,2,1,0:T(8,128)}), f32[4,4,8,128]{3,2,1,0:T(8,128)S(1)}, u32[]{:S(2)}, u32[]{:S(2)}) %all-to-all-start) | async-done | bytes 65568 | tf_op jit(solution)/shard_map/all_to_all | solution.py:84
  36.5 1.3 %collective-permute-start.1 = (bf16[1,1,8,128]{3,2,1,0:T(8,128)(2,1)S(1)}, bf16[1,1,8,128]{3,2,1,0:T(8,128)(2,1)S(1)}, u32[]{:S(2)}, u32[]{:S(2)}) collective-permute-start(bf16[1,1,8,128]{3,2,1,0:T(8,128)(2,1)S(1)} %get-tuple-element.12), channel_id=1, source_target_pairs={{2,0},{3,1},{6,4},{7,5},{10,8},{11,9},{14,12},{15,13},{18,16},{19,... | collective-permute-start | bytes 6152 | tf_op jit(solution)/shard_map/ppermute | solution.py:19
  37.8 4.5 %collective-permute-start = (bf16[1,1,8,128]{3,2,1,0:T(8,128)(2,1)S(1)}, bf16[1,1,8,128]{3,2,1,0:T(8,128)(2,1)S(1)}, u32[]{:S(2)}, u32[]{:S(2)}) collective-permute-start(bf16[1,1,8,128]{3,2,1,0:T(8,128)(2,1)S(1)} %get-tuple-element.11), channel_id=1, source_target_pairs={{0,2},{1,3},{4,6},{5,7},{8,10},{9,11},{12,14},{13,15},{16,18},{17,... | collective-permute-start | bytes 6152 | tf_op jit(solution)/shard_map/ppermute | solution.py:16
  42.4 1.3 %collective-permute-done = bf16[1,1,8,128]{3,2,1,0:T(8,128)(2,1)S(1)} collective-permute-done((bf16[1,1,8,128]{3,2,1,0:T(8,128)(2,1)S(1)}, bf16[1,1,8,128]{3,2,1,0:T(8,128)(2,1)S(1)}, u32[]{:S(2)}, u32[]{:S(2)}) %collective-permute-start) | collective-permute-done | bytes 2080 | tf_op jit(solution)/shard_map/ppermute | solution.py:16
  43.7 1.8 %all_gather.6 = bf16[1,6,8,256]{3,2,1,0:T(8,128)(2,1)S(1)} all-gather(bf16[1,6,8,128]{3,2,1,0:T(8,128)(2,1)S(1)} %pad_maximum_fusion), channel_id=1, replica_groups=mesh['groups'=2,'date'=4,'tile'=2,'head'=2] {'head'}, dimensions={3}, use_global_device_ids=true | all-gather | bytes 36864 | tf_op jit(solution)/shard_map/all_gather | solution.py:47
  46.7 1.3 %collective-permute-start.3 = (bf16[1,1,8,128]{3,2,1,0:T(8,128)(2,1)S(1)}, bf16[1,1,8,128]{3,2,1,0:T(8,128)(2,1)S(1)}, u32[]{:S(2)}, u32[]{:S(2)}) collective-permute-start(bf16[1,1,8,128]{3,2,1,0:T(8,128)(2,1)S(1)} %get-tuple-element.10), channel_id=1, source_target_pairs={{2,0},{3,1},{6,4},{7,5},{10,8},{11,9},{14,12},{15,13},{18,16},{19,... | collective-permute-start | bytes 6152 | tf_op jit(solution)/shard_map/ppermute | solution.py:19
  48.0 4.5 %collective-permute-start.2 = (bf16[1,1,8,128]{3,2,1,0:T(8,128)(2,1)S(1)}, bf16[1,1,8,128]{3,2,1,0:T(8,128)(2,1)S(1)}, u32[]{:S(2)}, u32[]{:S(2)}) collective-permute-start(bf16[1,1,8,128]{3,2,1,0:T(8,128)(2,1)S(1)} %get-tuple-element.9), channel_id=1, source_target_pairs={{0,2},{1,3},{4,6},{5,7},{8,10},{9,11},{12,14},{13,15},{16,18},{17,... | collective-permute-start | bytes 6152 | tf_op jit(solution)/shard_map/ppermute | solution.py:16
  52.6 1.3 %collective-permute-done.2 = bf16[1,1,8,128]{3,2,1,0:T(8,128)(2,1)S(1)} collective-permute-done((bf16[1,1,8,128]{3,2,1,0:T(8,128)(2,1)S(1)}, bf16[1,1,8,128]{3,2,1,0:T(8,128)(2,1)S(1)}, u32[]{:S(2)}, u32[]{:S(2)}) %collective-permute-start.2) | collective-permute-done | bytes 2080 | tf_op jit(solution)/shard_map/ppermute | solution.py:16
  53.9 1.8 %all_gather.7 = bf16[1,6,8,256]{3,2,1,0:T(8,128)(2,1)S(1)} all-gather(bf16[1,6,8,128]{3,2,1,0:T(8,128)(2,1)S(1)} %pad_maximum_fusion.1), channel_id=1, replica_groups=mesh['groups'=2,'date'=4,'tile'=2,'head'=2] {'head'}, dimensions={3}, use_global_device_ids=true | all-gather | bytes 36864 | tf_op jit(solution)/shard_map/all_gather | solution.py:47
  56.8 0.7 %fusion.3 = bf16[1,4,8,128]{3,2,1,0:T(8,128)(2,1)} fusion(f32[32,128]{1,0:T(8,128)S(1)} %convolution_add_fusion.1, bf16[3,3,256,128]{3,2,1,0:T(8,128)(2,1)S(1)} %copy-done.1, bf16[1,6,8,256]{3,2,1,0:T(8,128)(2,1)S(1)} %all_gather.7), kind=kOutput, calls=%fused_computation.22 | convolution fusion | flops 2105344 | bytes 114688 | tf_op jit(solution)/shard_map/dot_general | solution.py:53
  (46 shorter events, 3.5 us)
Async XLA Ops:
  6.0 7.8 %copy-start.2 = (bf16[256,128]{1,0:T(8,128)(2,1)S(1)}, bf16[256,128]{1,0:T(8,128)(2,1)}, u32[]{:S(2)}) copy-start(bf16[256,128]{1,0:T(8,128)(2,1)} %param.13) | copy-start | bytes 196612
  6.0 7.9 %copy-start.3 = (bf16[4,4,8,16,256]{4,3,2,1,0:T(8,128)(2,1)S(1)}, bf16[4,4,8,16,256]{4,3,2,1,0:T(8,128)(2,1)}, u32[]{:S(2)}) copy-start(bf16[4,4,8,16,256]{4,3,2,1,0:T(8,128)(2,1)} %param.8) | copy-start | bytes 3145732
  7.1 11.8 %all-to-all-start.1 = ((f32[4,1,128]{2,1,0:T(1,128)}), f32[4,1,128]{2,1,0:T(1,128)S(1)}, u32[]{:S(2)}, u32[]{:S(2)}) async-start(f32[4,1,128]{2,1,0:T(1,128)} %reshape.252), calls=%async_computation.1 | async-start | bytes 4096 | tf_op jit(solution)/shard_map/all_to_all | solution.py:82
  15.4 30.1 %copy-start = (bf16[3,3,256,128]{3,2,1,0:T(8,128)(2,1)S(1)}, bf16[3,3,256,128]{3,2,1,0:T(8,128)(2,1)}, u32[]{:S(2)}) copy-start(bf16[3,3,256,128]{3,2,1,0:T(8,128)(2,1)} %param.14) | copy-start | bytes 1769476
  18.9 8.6 %all-to-all-start.2 = ((f32[4,1,128]{2,1,0:T(1,128)}), f32[4,1,128]{2,1,0:T(1,128)S(1)}, u32[]{:S(2)}, u32[]{:S(2)}) async-start(f32[4,1,128]{2,1,0:T(1,128)} %reshape.250), calls=%async_computation.2 | async-start | bytes 4096 | tf_op jit(solution)/shard_map/all_to_all | solution.py:83
  27.5 9.0 %all-to-all-start = ((f32[4,4,8,128]{3,2,1,0:T(8,128)}), f32[4,4,8,128]{3,2,1,0:T(8,128)S(1)}, u32[]{:S(2)}, u32[]{:S(2)}) async-start(f32[4,4,8,128]{3,2,1,0:T(8,128)} %reshape.228), calls=%async_computation | async-start | bytes 131072 | tf_op jit(solution)/shard_map/all_to_all | solution.py:84
  31.9 23.8 %copy-start.1 = (bf16[3,3,256,128]{3,2,1,0:T(8,128)(2,1)S(1)}, bf16[3,3,256,128]{3,2,1,0:T(8,128)(2,1)}, u32[]{:S(2)}) copy-start(bf16[3,3,256,128]{3,2,1,0:T(8,128)(2,1)} %param.15) | copy-start | bytes 1769476
  36.5 5.9 %collective-permute-start.1 = (bf16[1,1,8,128]{3,2,1,0:T(8,128)(2,1)S(1)}, bf16[1,1,8,128]{3,2,1,0:T(8,128)(2,1)S(1)}, u32[]{:S(2)}, u32[]{:S(2)}) collective-permute-start(bf16[1,1,8,128]{3,2,1,0:T(8,128)(2,1)S(1)} %get-tuple-element.12), channel_id=1, source_target_pairs={{2,0},{3,1},{6,4},{7,5},{10,8},{11,9},{14,12},{15,13},{18,16},{19,... | collective-permute-start | bytes 6152 | tf_op jit(solution)/shard_map/ppermute | solution.py:19
  37.8 5.8 %collective-permute-start = (bf16[1,1,8,128]{3,2,1,0:T(8,128)(2,1)S(1)}, bf16[1,1,8,128]{3,2,1,0:T(8,128)(2,1)S(1)}, u32[]{:S(2)}, u32[]{:S(2)}) collective-permute-start(bf16[1,1,8,128]{3,2,1,0:T(8,128)(2,1)S(1)} %get-tuple-element.11), channel_id=1, source_target_pairs={{0,2},{1,3},{4,6},{5,7},{8,10},{9,11},{12,14},{13,15},{16,18},{17,... | collective-permute-start | bytes 6152 | tf_op jit(solution)/shard_map/ppermute | solution.py:16
  46.7 5.9 %collective-permute-start.3 = (bf16[1,1,8,128]{3,2,1,0:T(8,128)(2,1)S(1)}, bf16[1,1,8,128]{3,2,1,0:T(8,128)(2,1)S(1)}, u32[]{:S(2)}, u32[]{:S(2)}) collective-permute-start(bf16[1,1,8,128]{3,2,1,0:T(8,128)(2,1)S(1)} %get-tuple-element.10), channel_id=1, source_target_pairs={{2,0},{3,1},{6,4},{7,5},{10,8},{11,9},{14,12},{15,13},{18,16},{19,... | collective-permute-start | bytes 6152 | tf_op jit(solution)/shard_map/ppermute | solution.py:19
  48.0 5.8 %collective-permute-start.2 = (bf16[1,1,8,128]{3,2,1,0:T(8,128)(2,1)S(1)}, bf16[1,1,8,128]{3,2,1,0:T(8,128)(2,1)S(1)}, u32[]{:S(2)}, u32[]{:S(2)}) collective-permute-start(bf16[1,1,8,128]{3,2,1,0:T(8,128)(2,1)S(1)} %get-tuple-element.9), channel_id=1, source_target_pairs={{0,2},{1,3},{4,6},{5,7},{8,10},{9,11},{12,14},{13,15},{16,18},{17,... | collective-permute-start | bytes 6152 | tf_op jit(solution)/shard_map/ppermute | solution.py:16
where the time goes:
time: 58.1 us; the launch traced here: 57.5 us
  starting transfers between devices  24.5 us (42%)
  waiting for transfers between devices  12.6 us (22%)
  matrix products  7.09 us (12%)
  local copies, waits for them, and re-layouts  5.82 us (10%)
  other arithmetic  3.7 us (6%)
  blocking collectives  3.62 us (6%)
    ppermute x2, starting transfers between devices, with_halo(): lax.ppermute(lax.slice_in_dim(block, block.shape[dim] - width, None, axis...  9.08 us
    all_to_all x1, starting transfers between devices, local(): lax.all_to_all(top, 'date', split_axis=0, concat_axis=0, tiled=True)  6.32 us
    all_to_all x1, waiting for transfers between devices, local(): lax.all_to_all(totals, 'date', split_axis=0, concat_axis=0, tiled=True)  4.08 us
    all_to_all x1, waiting for transfers between devices, local(): lax.all_to_all(sums, 'date', split_axis=0, concat_axis=0, tiled=True)  4.05 us
    all_gather x2, blocking collectives, convolve(): whole = lax.all_gather(padded, 'head', axis=3, tiled=True)  3.62 us
    all_to_all x1, starting transfers between devices, local(): lax.all_to_all(sums, 'date', split_axis=0, concat_axis=0, tiled=True)  3.28 us
    all_to_all x1, starting transfers between devices, local(): lax.all_to_all(totals, 'date', split_axis=0, concat_axis=0, tiled=True)  3.2 us
    dot_general x18, matrix products, convolve(): jnp.dot(piece, kernel[arow, bcol], preferred_element_type=jnp.float32)  3.05 us
  transfers between devices with their start and end apart: 7, of which 5 were waited for; matrix products, arithmetic and copies ran while one was open for 11% of the time, Pallas kernels for 0%

commit v1 on v0

--- a/solution.py
+++ b/solution.py
@@ -6,6 +6,28 @@
 HSIZE = 32
 TILE_DEV = 1
 cloud_penalty = 6.0
+
+
+def cut_along(x, dim, peers):
+    before, after = (x.shape[:dim], x.shape[dim + 1 :])
+    return jnp.moveaxis(x.reshape(*before, peers, -1, *after), dim, 0)
+
+
+def joined_along(blocks, dim):
+    shape = list(blocks.shape[1:])
+    shape[dim] *= blocks.shape[0]
+    return jnp.moveaxis(blocks, 0, dim).reshape(shape)
+
+
+def swapped_with_each(x, axis, split_dim, concat_dim):
+    size, position = (lax.axis_size(axis), lax.axis_index(axis))
+    blocks = cut_along(x, split_dim, size)
+    outs = [blocks[position]]
+    for lap in range(1, size):
+        sent = blocks[position ^ lap]
+        outs.append(lax.ppermute(sent, axis, [(i, i ^ lap) for i in range(size)]))
+    blocks = jnp.stack(outs)[position ^ jnp.arange(size)]
+    return joined_along(blocks, concat_dim)
 
 
 def with_halo(block, sides, width):
@@ -81,7 +103,7 @@
     got = (
         lax.all_to_all(top, "date", split_axis=0, concat_axis=0, tiled=True),
         lax.all_to_all(totals, "date", split_axis=0, concat_axis=0, tiled=True),
-        lax.all_to_all(sums, "date", split_axis=0, concat_axis=0, tiled=True),
+        swapped_with_each(sums, "date", 0, 0),
     )
     sources = got[0].shape[0] // TILE_DEV
     tops = got[0].reshape(sources, TILE_DEV, rows, cols, heads_dev)

time: 58.1 us -> 55.2 us (0.950)
  waiting for transfers between devices: 12.6 us -> 6.67 us
  starting transfers between devices: 24.5 us -> 27.5 us
    ppermute x0 -> x3, starting transfers between devices: none -> 4.53 us  [swapped_with_each(): outs.append(lax.ppermute(sent, axis, [(i, i ^ lap) for i in range(size)]))]
    all_to_all x1 -> x0, waiting for transfers between devices: 4.05 us -> none  [local(): lax.all_to_all(sums, 'date', split_axis=0, concat_axis=0, tiled=True)]
    all_to_all x1 -> x0, starting transfers between devices: 3.28 us -> none  [local(): lax.all_to_all(sums, 'date', split_axis=0, concat_axis=0, tiled=True)]
    all_to_all x1, waiting for transfers between devices: 1.89 us -> 0.01 us  [local(): lax.all_to_all(top, 'date', split_axis=0, concat_axis=0, tiled=True)]
    all_to_all x1, starting transfers between devices: 3.2 us -> 5.01 us  [local(): lax.all_to_all(totals, 'date', split_axis=0, concat_axis=0, tiled=True)]
    reshape x1 -> x0, local copies, waits for them, and re-layouts: 0.78 us -> none  [local(): jnp.sum(expo[..., None] * vals, axis=3)]
  transfers between devices with their start and end apart: 7 -> 9, of which waited for: 5 -> 3; matrix products, arithmetic and copies ran while one was open for 11% -> 11% of each run, Pallas kernels for 0% -> 0%
where the time goes in v1:
time: 55.2 us; the launch traced here: 54.7 us
  starting transfers between devices  27.5 us (50%)
  matrix products  7.09 us (13%)
  waiting for transfers between devices  6.67 us (12%)
  local copies, waits for them, and re-layouts  5.8 us (11%)
  other arithmetic  3.72 us (7%)
  blocking collectives  3.62 us (7%)
    ppermute x2, starting transfers between devices, with_halo(): lax.ppermute(lax.slice_in_dim(block, block.shape[dim] - width, None, axis...  9.08 us
    all_to_all x1, starting transfers between devices, local(): lax.all_to_all(top, 'date', split_axis=0, concat_axis=0, tiled=True)  6.32 us
    all_to_all x1, starting transfers between devices, local(): lax.all_to_all(totals, 'date', split_axis=0, concat_axis=0, tiled=True)  5.01 us
    ppermute x3, starting transfers between devices, swapped_with_each(): outs.append(lax.ppermute(sent, axis, [(i, i ^ lap) for i in range(size)]))  4.53 us
    all_to_all x1, waiting for transfers between devices, local(): lax.all_to_all(totals, 'date', split_axis=0, concat_axis=0, tiled=True)  4.09 us
    all_gather x2, blocking collectives, convolve(): whole = lax.all_gather(padded, 'head', axis=3, tiled=True)  3.62 us
    dot_general x18, matrix products, convolve(): jnp.dot(piece, kernel[arow, bcol], preferred_element_type=jnp.float32)  3.05 us
    unnamed x14, local copies, waits for them, and re-layouts  2.67 us
  transfers between devices with their start and end apart: 9, of which 3 were waited for; matrix products, arithmetic and copies ran while one was open for 11% of the time, Pallas kernels for 0%

profile of v1, /device:TPU:0, one launch (start us, length us, event | category | flops | bytes accessed | tf_op | source)
XLA Modules:
  0.0 54.7 jit_solution(135719271481528787)
XLA Ops:
  0.0 0.9 %copy.23 = bf16[256,128]{0,1:T(8,128)(2,1)S(1)} copy(bf16[256,128]{1,0:T(8,128)(2,1)} %param.12) | data formatting | bytes 131072 | tf_op args[4]
  1.0 0.7 %mul.71 = f32[4,32]{1,0:T(4,128)S(1)} reshape(f32[128]{0:T(128)} %param.11) | data formatting | bytes 1024 | tf_op jit(solution)/shard_map/mul | solution.py:97
  1.7 0.7 %convert_element_type.63 = f32[16]{0:T(128)S(1)} convert(s32[16]{0:T(128)} %param.10) | non-fusion elementwise | flops 16 | bytes 128 | tf_op jit(solution)/shard_map/convert_element_type | solution.py:50
  2.4 0.8 %subtract_multiply_fusion = f32[4,4,8,16]{3,2,1,0:T(8,128)S(1)} fusion(s32[4,4,8,16]{3,2,1,0:T(8,128)} %param.9), kind=kLoop, calls=%fused_computation.82 | loop fusion | flops 6144 | bytes 16384 | tf_op jit(solution)/shard_map/mul | solution.py:98
  3.4 2.6 %multiply_reduce_fusion.1 = f32[4,4,8,16,4]{3,4,2,1,0:T(4,128)S(1)} fusion(bf16[4,32,256,1,1,1]{2,1,0,5,4,3:T(8,128)(2,1)S(1)} %bitcast.164, f32[4,32]{1,0:T(4,128)S(1)} %mul.71, bf16[4,4,8,16,256]{4,3,2,1,0:T(8,128)(2,1)} %param.8, f32[16,256]{1,0:T(8,128)S(1)} %fusion.48), kind=kOutput, calls=%fused_computation.2 | convolution fusion | flops 136306688 | bytes 1163776 | tf_op jit(solution)/shard_map/dot_general | solution.py:90
  6.0 0.2 fusion.8
  6.3 0.2 copy.25
  6.4 0.7 %reshape.299 = f32[4,1,128]{2,1,0:T(1,128)} reshape(f32[4,4,4,8]{3,2,1,0:T(4,128)S(1)} %bitcast.163) | data formatting | bytes 4096
  7.1 6.3 %all-to-all-start = ((f32[4,1,128]{2,1,0:T(1,128)}), f32[4,1,128]{2,1,0:T(1,128)S(1)}, u32[]{:S(2)}, u32[]{:S(2)}) async-start(f32[4,1,128]{2,1,0:T(1,128)} %reshape.299), calls=%async_computation | async-start | bytes 4096 | tf_op jit(solution)/shard_map/all_to_all | solution.py:104
  13.4 0.4 fusion.94
  14.0 1.4 %multiply_reduce_fusion = f32[4,4,8,4,32]{4,3,2,1,0:T(4,128)S(1)} fusion(bf16[4,32,256,1,1,1]{2,1,0,5,4,3:T(8,128)(2,1)S(1)} %bitcast.165, f32[4,4,8,16,4]{3,4,2,1,0:T(4,128)S(1)} %get-tuple-element.8, bf16[4,4,8,16,256]{4,3,2,1,0:T(8,128)(2,1)S(1)} %copy-done.3, f32[16,256]{1,0:T(8,128)S(1)} %fusion.48), kind=kOutput, calls=%fused_computation.1 | convolution fusion | flops 136298496 | bytes 1228800 | tf_op jit(solution)/shard_map/dot_general | solution.py:93
  15.6 3.9 %collective-permute-start.2 = (f32[1,4,8,128]{3,2,1,0:T(8,128)S(1)}, f32[1,4,8,128]{3,2,1,0:T(8,128)S(1)}, u32[]{:S(2)}, u32[]{:S(2)}) collective-permute-start(f32[1,4,8,128]{3,2,1,0:T(8,128)S(1)} %get-tuple-element.10), channel_id=1, source_target_pairs={{0,12},{4,8},{8,4},{12,0},{1,13},{5,9},{9,5},{13,1},{2,14},{6,10},... | collective-permute-start | bytes 49160 | tf_op jit(solution)/shard_map/ppermute | solution.py:28
  19.5 0.6 %collective-permute-start = (f32[1,4,8,128]{3,2,1,0:T(8,128)S(1)}, f32[1,4,8,128]{3,2,1,0:T(8,128)S(1)}, u32[]{:S(2)}, u32[]{:S(2)}) collective-permute-start(f32[1,4,8,128]{3,2,1,0:T(8,128)S(1)} %get-tuple-element.12), channel_id=1, source_target_pairs={{0,4},{4,0},{8,12},{12,8},{1,5},{5,1},{9,13},{13,9},{2,6},{6,2},{1... | collective-permute-start | bytes 49160 | tf_op jit(solution)/shard_map/ppermute | solution.py:28
  20.2 0.2 copy.27
  20.3 0.7 %reshape.297 = f32[4,1,128]{2,1,0:T(1,128)} reshape(f32[4,4,4,8]{3,2,1,0:T(4,128)S(1)} %bitcast.162) | data formatting | bytes 4096
  21.0 5.0 %all-to-all-start.1 = ((f32[4,1,128]{2,1,0:T(1,128)}), f32[4,1,128]{2,1,0:T(1,128)S(1)}, u32[]{:S(2)}, u32[]{:S(2)}) async-start(f32[4,1,128]{2,1,0:T(1,128)} %reshape.297), calls=%async_computation.1 | async-start | bytes 4096 | tf_op jit(solution)/shard_map/all_to_all | solution.py:105
  26.0 0.5 broadcast.181
  26.6 0.7 %reduce.9 = f32[4,128]{1,0:T(4,128)S(1)} reduce(f32[4,1,128]{2,1,0:T(1,128)S(1)} %all-to-all-done, f32[]{:T(128)} %broadcast.181), dimensions={1}, to_apply=%all_to_all.6.reduce_sub_computation | reduce | bytes 4100 | tf_op jit(solution)/shard_map/all_to_all | solution.py:104
  27.4 4.1 %all-to-all-done.1 = f32[4,1,128]{2,1,0:T(1,128)S(1)} async-done(((f32[4,1,128]{2,1,0:T(1,128)}), f32[4,1,128]{2,1,0:T(1,128)S(1)}, u32[]{:S(2)}, u32[]{:S(2)}) %all-to-all-start.1) | async-done | bytes 2080 | tf_op jit(solution)/shard_map/all_to_all | solution.py:105
  31.4 0.7 %reduce.10 = f32[4,128]{1,0:T(4,128)S(1)} reduce(f32[4,1,128]{2,1,0:T(1,128)S(1)} %all-to-all-done.1, f32[]{:T(128)} %broadcast.181), dimensions={1}, to_apply=%all_to_all.7.reduce_sub_computation | reduce | bytes 4100 | tf_op jit(solution)/shard_map/all_to_all | solution.py:105
  32.5 0.2 copy.26
  32.7 0.2 broadcast_in_dim.28
  33.1 0.6 %gather_fusion = f32[4,4,8,128]{3,2,1,0:T(8,128)S(1)} fusion(f32[4,4,8,128]{3,2,1,0:T(8,128)S(1)} %maximum_bitcast_fusion, s32[1024]{0:T(1024)S(1)} %pad_clamp_fusion), kind=kCustom, calls=%fused_computation | custom fusion | bytes 131088 | tf_op jit(solution)/shard_map/gather | solution.py:29
  33.8 1.3 %collective-permute-start.4 = (bf16[1,1,8,128]{3,2,1,0:T(8,128)(2,1)S(1)}, bf16[1,1,8,128]{3,2,1,0:T(8,128)(2,1)S(1)}, u32[]{:S(2)}, u32[]{:S(2)}) collective-permute-start(bf16[1,1,8,128]{3,2,1,0:T(8,128)(2,1)S(1)} %get-tuple-element.16), channel_id=1, source_target_pairs={{2,0},{3,1},{6,4},{7,5},{10,8},{11,9},{14,12},{15,13},{18,16},{19,... | collective-permute-start | bytes 6152 | tf_op jit(solution)/shard_map/ppermute | solution.py:41
  35.1 4.5 %collective-permute-start.3 = (bf16[1,1,8,128]{3,2,1,0:T(8,128)(2,1)S(1)}, bf16[1,1,8,128]{3,2,1,0:T(8,128)(2,1)S(1)}, u32[]{:S(2)}, u32[]{:S(2)}) collective-permute-start(bf16[1,1,8,128]{3,2,1,0:T(8,128)(2,1)S(1)} %get-tuple-element.15), channel_id=1, source_target_pairs={{0,2},{1,3},{4,6},{5,7},{8,10},{9,11},{12,14},{13,15},{16,18},{17,... | collective-permute-start | bytes 6152 | tf_op jit(solution)/shard_map/ppermute | solution.py:38
  39.6 1.3 %collective-permute-done.3 = bf16[1,1,8,128]{3,2,1,0:T(8,128)(2,1)S(1)} collective-permute-done((bf16[1,1,8,128]{3,2,1,0:T(8,128)(2,1)S(1)}, bf16[1,1,8,128]{3,2,1,0:T(8,128)(2,1)S(1)}, u32[]{:S(2)}, u32[]{:S(2)}) %collective-permute-start.3) | collective-permute-done | bytes 2080 | tf_op jit(solution)/shard_map/ppermute | solution.py:38
  40.9 1.8 %all_gather.6 = bf16[1,6,8,256]{3,2,1,0:T(8,128)(2,1)S(1)} all-gather(bf16[1,6,8,128]{3,2,1,0:T(8,128)(2,1)S(1)} %pad_maximum_fusion), channel_id=1, replica_groups=mesh['groups'=2,'date'=4,'tile'=2,'head'=2] {'head'}, dimensions={3}, use_global_device_ids=true | all-gather | bytes 36864 | tf_op jit(solution)/shard_map/all_gather | solution.py:69
  43.9 1.3 %collective-permute-start.6 = (bf16[1,1,8,128]{3,2,1,0:T(8,128)(2,1)S(1)}, bf16[1,1,8,128]{3,2,1,0:T(8,128)(2,1)S(1)}, u32[]{:S(2)}, u32[]{:S(2)}) collective-permute-start(bf16[1,1,8,128]{3,2,1,0:T(8,128)(2,1)S(1)} %get-tuple-element.14), channel_id=1, source_target_pairs={{2,0},{3,1},{6,4},{7,5},{10,8},{11,9},{14,12},{15,13},{18,16},{19,... | collective-permute-start | bytes 6152 | tf_op jit(solution)/shard_map/ppermute | solution.py:41
  45.2 4.5 %collective-permute-start.5 = (bf16[1,1,8,128]{3,2,1,0:T(8,128)(2,1)S(1)}, bf16[1,1,8,128]{3,2,1,0:T(8,128)(2,1)S(1)}, u32[]{:S(2)}, u32[]{:S(2)}) collective-permute-start(bf16[1,1,8,128]{3,2,1,0:T(8,128)(2,1)S(1)} %get-tuple-element.13), channel_id=1, source_target_pairs={{0,2},{1,3},{4,6},{5,7},{8,10},{9,11},{12,14},{13,15},{16,18},{17,... | collective-permute-start | bytes 6152 | tf_op jit(solution)/shard_map/ppermute | solution.py:38
  49.8 1.3 %collective-permute-done.5 = bf16[1,1,8,128]{3,2,1,0:T(8,128)(2,1)S(1)} collective-permute-done((bf16[1,1,8,128]{3,2,1,0:T(8,128)(2,1)S(1)}, bf16[1,1,8,128]{3,2,1,0:T(8,128)(2,1)S(1)}, u32[]{:S(2)}, u32[]{:S(2)}) %collective-permute-start.5) | collective-permute-done | bytes 2080 | tf_op jit(solution)/shard_map/ppermute | solution.py:38
  51.1 1.8 %all_gather.7 = bf16[1,6,8,256]{3,2,1,0:T(8,128)(2,1)S(1)} all-gather(bf16[1,6,8,128]{3,2,1,0:T(8,128)(2,1)S(1)} %pad_maximum_fusion.1), channel_id=1, replica_groups=mesh['groups'=2,'date'=4,'tile'=2,'head'=2] {'head'}, dimensions={3}, use_global_device_ids=true | all-gather | bytes 36864 | tf_op jit(solution)/shard_map/all_gather | solution.py:69
  54.0 0.7 %fusion.3 = bf16[1,4,8,128]{3,2,1,0:T(8,128)(2,1)} fusion(f32[32,128]{1,0:T(8,128)S(1)} %convolution_add_fusion.1, bf16[3,3,256,128]{3,2,1,0:T(8,128)(2,1)S(1)} %copy-done.1, bf16[1,6,8,256]{3,2,1,0:T(8,128)(2,1)S(1)} %all_gather.7), kind=kOutput, calls=%fused_computation.23 | convolution fusion | flops 2105344 | bytes 114688 | tf_op jit(solution)/shard_map/dot_general | solution.py:75
  (55 shorter events, 3.6 us)
Async XLA Ops:
  6.0 7.9 %copy-start.2 = (bf16[256,128]{1,0:T(8,128)(2,1)S(1)}, bf16[256,128]{1,0:T(8,128)(2,1)}, u32[]{:S(2)}) copy-start(bf16[256,128]{1,0:T(8,128)(2,1)} %param.13) | copy-start | bytes 196612
  6.0 8.0 %copy-start.3 = (bf16[4,4,8,16,256]{4,3,2,1,0:T(8,128)(2,1)S(1)}, bf16[4,4,8,16,256]{4,3,2,1,0:T(8,128)(2,1)}, u32[]{:S(2)}) copy-start(bf16[4,4,8,16,256]{4,3,2,1,0:T(8,128)(2,1)} %param.8) | copy-start | bytes 3145732
  7.1 13.9 %all-to-all-start = ((f32[4,1,128]{2,1,0:T(1,128)}), f32[4,1,128]{2,1,0:T(1,128)S(1)}, u32[]{:S(2)}, u32[]{:S(2)}) async-start(f32[4,1,128]{2,1,0:T(1,128)} %reshape.299), calls=%async_computation | async-start | bytes 4096 | tf_op jit(solution)/shard_map/all_to_all | solution.py:104
  15.6 27.2 %copy-start = (bf16[3,3,256,128]{3,2,1,0:T(8,128)(2,1)S(1)}, bf16[3,3,256,128]{3,2,1,0:T(8,128)(2,1)}, u32[]{:S(2)}) copy-start(bf16[3,3,256,128]{3,2,1,0:T(8,128)(2,1)} %param.14) | copy-start | bytes 1769476
  15.6 17.5 %collective-permute-start.2 = (f32[1,4,8,128]{3,2,1,0:T(8,128)S(1)}, f32[1,4,8,128]{3,2,1,0:T(8,128)S(1)}, u32[]{:S(2)}, u32[]{:S(2)}) collective-permute-start(f32[1,4,8,128]{3,2,1,0:T(8,128)S(1)} %get-tuple-element.10), channel_id=1, source_target_pairs={{0,12},{4,8},{8,4},{12,0},{1,13},{5,9},{9,5},{13,1},{2,14},{6,10},... | collective-permute-start | bytes 49160 | tf_op jit(solution)/shard_map/ppermute | solution.py:28
  19.5 13.6 %collective-permute-start.1 = (f32[1,4,8,128]{3,2,1,0:T(8,128)S(1)}, f32[1,4,8,128]{3,2,1,0:T(8,128)S(1)}, u32[]{:S(2)}, u32[]{:S(2)}) collective-permute-start(f32[1,4,8,128]{3,2,1,0:T(8,128)S(1)} %get-tuple-element.11), channel_id=1, source_target_pairs={{0,8},{4,12},{8,0},{12,4},{1,9},{5,13},{9,1},{13,5},{2,10},{6,14},... | collective-permute-start | bytes 49160 | tf_op jit(solution)/shard_map/ppermute | solution.py:28
  19.5 13.6 %collective-permute-start = (f32[1,4,8,128]{3,2,1,0:T(8,128)S(1)}, f32[1,4,8,128]{3,2,1,0:T(8,128)S(1)}, u32[]{:S(2)}, u32[]{:S(2)}) collective-permute-start(f32[1,4,8,128]{3,2,1,0:T(8,128)S(1)} %get-tuple-element.12), channel_id=1, source_target_pairs={{0,4},{4,0},{8,12},{12,8},{1,5},{5,1},{9,13},{13,9},{2,6},{6,2},{1... | collective-permute-start | bytes 49160 | tf_op jit(solution)/shard_map/ppermute | solution.py:28
  21.0 10.4 %all-to-all-start.1 = ((f32[4,1,128]{2,1,0:T(1,128)}), f32[4,1,128]{2,1,0:T(1,128)S(1)}, u32[]{:S(2)}, u32[]{:S(2)}) async-start(f32[4,1,128]{2,1,0:T(1,128)} %reshape.297), calls=%async_computation.1 | async-start | bytes 4096 | tf_op jit(solution)/shard_map/all_to_all | solution.py:105
  32.9 20.0 %copy-start.1 = (bf16[3,3,256,128]{3,2,1,0:T(8,128)(2,1)S(1)}, bf16[3,3,256,128]{3,2,1,0:T(8,128)(2,1)}, u32[]{:S(2)}) copy-start(bf16[3,3,256,128]{3,2,1,0:T(8,128)(2,1)} %param.15) | copy-start | bytes 1769476
  33.8 5.9 %collective-permute-start.4 = (bf16[1,1,8,128]{3,2,1,0:T(8,128)(2,1)S(1)}, bf16[1,1,8,128]{3,2,1,0:T(8,128)(2,1)S(1)}, u32[]{:S(2)}, u32[]{:S(2)}) collective-permute-start(bf16[1,1,8,128]{3,2,1,0:T(8,128)(2,1)S(1)} %get-tuple-element.16), channel_id=1, source_target_pairs={{2,0},{3,1},{6,4},{7,5},{10,8},{11,9},{14,12},{15,13},{18,16},{19,... | collective-permute-start | bytes 6152 | tf_op jit(solution)/shard_map/ppermute | solution.py:41
  35.1 5.8 %collective-permute-start.3 = (bf16[1,1,8,128]{3,2,1,0:T(8,128)(2,1)S(1)}, bf16[1,1,8,128]{3,2,1,0:T(8,128)(2,1)S(1)}, u32[]{:S(2)}, u32[]{:S(2)}) collective-permute-start(bf16[1,1,8,128]{3,2,1,0:T(8,128)(2,1)S(1)} %get-tuple-element.15), channel_id=1, source_target_pairs={{0,2},{1,3},{4,6},{5,7},{8,10},{9,11},{12,14},{13,15},{16,18},{17,... | collective-permute-start | bytes 6152 | tf_op jit(solution)/shard_map/ppermute | solution.py:38
  43.9 5.9 %collective-permute-start.6 = (bf16[1,1,8,128]{3,2,1,0:T(8,128)(2,1)S(1)}, bf16[1,1,8,128]{3,2,1,0:T(8,128)(2,1)S(1)}, u32[]{:S(2)}, u32[]{:S(2)}) collective-permute-start(bf16[1,1,8,128]{3,2,1,0:T(8,128)(2,1)S(1)} %get-tuple-element.14), channel_id=1, source_target_pairs={{2,0},{3,1},{6,4},{7,5},{10,8},{11,9},{14,12},{15,13},{18,16},{19,... | collective-permute-start | bytes 6152 | tf_op jit(solution)/shard_map/ppermute | solution.py:41
  45.2 5.8 %collective-permute-start.5 = (bf16[1,1,8,128]{3,2,1,0:T(8,128)(2,1)S(1)}, bf16[1,1,8,128]{3,2,1,0:T(8,128)(2,1)S(1)}, u32[]{:S(2)}, u32[]{:S(2)}) collective-permute-start(bf16[1,1,8,128]{3,2,1,0:T(8,128)(2,1)S(1)} %get-tuple-element.13), channel_id=1, source_target_pairs={{0,2},{1,3},{4,6},{5,7},{8,10},{9,11},{12,14},{13,15},{16,18},{17,... | collective-permute-start | bytes 6152 | tf_op jit(solution)/shard_map/ppermute | solution.py:38
